TPU v7x, 32 devices: a whole 2x2x4 slice. The times are simulated.
32 devices in a mesh: seq: 8 (over y, x, core), dp: 4 (over z).
Axes of the slice: x: 2, y: 2, z: 4, core: 2. Of those that a mesh axis runs over, the one named last changes fastest.
Arguments:
- tokens: bfloat16 [8, 1024, 767], P('dp', 'seq'), may hold values from -6 to 6
- doc_lengths: int32 [8, 4], P('dp'), may hold values from 16 to 976, as said below
- first_gain: bfloat16 [767], replicated, may hold values from 0.25 to 1.75
- inward_weight: bfloat16 [767, 2304], replicated, may hold values from -0.21875 to 0.21875
- inward_bias: bfloat16 [2, 768], replicated, may hold values from -3 to 3
- outward_weight: bfloat16 [768, 767], replicated, may hold values from -0.875 to 0.875
- outward_bias: bfloat16 [767], replicated, may hold values from -2 to 2
- second_gain: bfloat16 [767], replicated, may hold values from 0.25 to 1.75
- up_weight: bfloat16 [767, 3072], replicated, may hold values from -0.21875 to 0.21875
- up_bias: bfloat16 [3072], replicated, may hold values from -3 to 3
- down_weight: bfloat16 [3072, 767], replicated, may hold values from -0.109375 to 0.109375
- down_bias: bfloat16 [767], replicated, may hold values from -2 to 2
- cotangent: bfloat16 [8, 1024, 767], P('dp', 'seq'), may hold values from -6 to 6
Outputs:
- output_tokens: bfloat16 [8, 1024, 767], P('dp', 'seq')
- grad_tokens: bfloat16 [8, 1024, 767], P('dp', 'seq')
- gain_first: float32 [767], replicated
- grad_inward: float32 [767, 2304], P(None, ('seq', 'dp'))
- bias_inward: float32 [2, 768], replicated
- grad_outward: float32 [768, 767], P(('seq', 'dp'))
- bias_outward: float32 [767], replicated
- gain_second: float32 [767], replicated
- grad_up: float32 [767, 3072], P(None, ('seq', 'dp'))
- bias_up: float32 [3072], replicated
- grad_down: float32 [3072, 767], P(('seq', 'dp'))
- bias_down: float32 [767], replicated
Inputs may be any that keep to these rules, and one draw needn't show every extreme that they name: `doc_lengths`: in each row the 4 lengths sum to 1024; one of them exceeds 1024 - 128, and which one is drawn.
All inputs are finite; a program needn't handle non-finite values.
Results may differ from a plain program's by a relative error of at most 0.013.
Values may be sent and summed in bfloat16 or wider, within the bound.
No kernel may reach another device: no remote copies, remote signals or barrier semaphores. Data moves between devices by JAX's collectives and lax.ppermute only.
A program may use at most 192 MiB of HBM per device.

v0:
```python
import math

import jax
import jax.numpy as jnp
from jax import lax
from jax.sharding import PartitionSpec as P

HEADS = 12
HEAD_DIM = 64


EPSILON = 1e-05
FLOOR = -1e30


def compressed_norm(values, gain_row):
    squares = jnp.sum(values * values, axis=-1, keepdims=True)
    totals = jnp.sum(values, axis=-1, keepdims=True)
    full_width = values.shape[-1] + 1
    return values * gain_row * lax.rsqrt((squares + totals * totals) / full_width + EPSILON)


def document_ids(doc_lengths, positions):
    doc_ends = jnp.cumsum(doc_lengths, axis=-1)
    return jnp.sum((positions[..., :, None] >= doc_ends[..., None, :]).astype(jnp.int32), axis=-1)


def block_masks(doc_lengths, query_pos, key_pos):
    query_ids = document_ids(doc_lengths, query_pos[None, :])
    key_ids = document_ids(doc_lengths, key_pos[None, :])
    same_doc = query_ids[:, :, None] == key_ids[:, None, :]
    causal = key_pos[None, None, :] <= query_pos[None, :, None]
    return (same_doc & causal)[:, :, None, :]


def blockwise(visit_block, running, pieces):
    piece_len = pieces[0].shape[1]
    step_len = math.gcd(piece_len, 1024)

    def one_block(block_index, current):
        block_start = block_index * step_len
        blocks = tuple(
            (lax.dynamic_slice_in_dim(member, block_start, step_len, 1) for member in pieces)
        )
        return visit_block(current, blocks, block_start)

    return lax.fori_loop(0, piece_len // step_len, one_block, running)


def local(
    tokens,
    doc_lengths,
    first_gain,
    inward_weight,
    inward_bias,
    outward_weight,
    outward_bias,
    second_gain,
    up_weight,
    up_bias,
    down_weight,
    down_bias,
    cotangent,
):
    batches, local_len = (tokens.shape[0], tokens.shape[1])
    head_width = inward_weight.shape[1] // 3
    score_scale = HEAD_DIM ** (-0.5)
    query_pos = lax.axis_index("seq") * local_len + jnp.arange(local_len, dtype=jnp.int32)
    token_values = tokens.astype(jnp.float32)
    norm_gain_one = first_gain.astype(jnp.float32)
    norm_gain_two = second_gain.astype(jnp.float32)
    normed_one = compressed_norm(token_values, norm_gain_one).astype(jnp.bfloat16)
    projected = jnp.einsum(
        "btd,df->btf", normed_one, inward_weight, preferred_element_type=jnp.float32
    )
    heads_shape = (batches, local_len, HEADS, HEAD_DIM)
    queries_low = (
        (projected[..., :head_width] + inward_bias[0].astype(jnp.float32))
        .astype(jnp.bfloat16)
        .reshape(heads_shape)
    )
    keys_low = projected[..., head_width : 2 * head_width].astype(jnp.bfloat16).reshape(heads_shape)
    values_low = (
        (projected[..., 2 * head_width :] + inward_bias[1].astype(jnp.float32))
        .astype(jnp.bfloat16)
        .reshape(heads_shape)
    )

    def forward_block(current, blocks, key_start):
        keys_block, values_block = (blocks[0], blocks[1])
        key_pos = key_start + jnp.arange(keys_block.shape[1], dtype=jnp.int32)
        allowed = block_masks(doc_lengths, query_pos, key_pos)
        accumulated, row_max, row_sum = current
        scores = (
            jnp.einsum(
                "bqhe,bkhe->bqhk", queries_low, keys_block, preferred_element_type=jnp.float32
            )
            * score_scale
        )
        scores = jnp.where(allowed, scores, FLOOR)
        new_max = jnp.maximum(row_max, jnp.max(scores, axis=-1))
        factor = jnp.exp(row_max - new_max)
        weights = jnp.where(allowed, jnp.exp(scores - new_max[..., None]), 0.0)
        row_sum = row_sum * factor + jnp.sum(weights, axis=-1)
        accumulated = accumulated * factor[..., None] + jnp.einsum(
            "bqhk,bkhe->bqhe",
            weights.astype(jnp.bfloat16),
            values_block,
            preferred_element_type=jnp.float32,
        )
        return (accumulated, new_max, row_sum)

    start_state = (
        jnp.zeros(heads_shape, jnp.float32),
        jnp.full(heads_shape[:3], FLOOR, jnp.float32),
        jnp.zeros(heads_shape[:3], jnp.float32),
    )
    accumulated, row_max, row_sum = blockwise(
        forward_block,
        start_state,
        (
            lax.all_gather(keys_low, "seq", axis=1, tiled=True),
            lax.all_gather(values_low, "seq", axis=1, tiled=True),
        ),
    )
    attended = accumulated / row_sum[..., None]
    log_total = row_max + jnp.log(row_sum)
    attended_low = attended.reshape(batches, local_len, head_width).astype(jnp.bfloat16)
    branch = jnp.einsum(
        "btf,fd->btd", attended_low, outward_weight, preferred_element_type=jnp.float32
    ) + outward_bias.astype(jnp.float32)
    residual = token_values + branch
    normed_two = compressed_norm(residual, norm_gain_two).astype(jnp.bfloat16)
    upward = jnp.einsum(
        "btd,df->btf", normed_two, up_weight, preferred_element_type=jnp.float32
    ) + up_bias.astype(jnp.float32)
    active_low = jax.nn.gelu(upward).astype(jnp.bfloat16)
    mlp_branch = jnp.einsum(
        "btf,fd->btd", active_low, down_weight, preferred_element_type=jnp.float32
    ) + down_bias.astype(jnp.float32)
    output_tokens = (residual + mlp_branch).astype(jnp.bfloat16)
    grad_output = cotangent.astype(jnp.float32)
    grad_down = jnp.einsum("btf,btd->fd", active_low, cotangent, preferred_element_type=jnp.float32)
    bias_down = jnp.sum(grad_output, axis=(0, 1))
    grad_active = jnp.einsum(
        "btd,fd->btf", cotangent, down_weight, preferred_element_type=jnp.float32
    )
    unused, gelu_back = jax.vjp(jax.nn.gelu, upward)
    grad_upward = gelu_back(grad_active)[0].astype(jnp.bfloat16)
    grad_up = jnp.einsum("btd,btf->df", normed_two, grad_upward, preferred_element_type=jnp.float32)
    bias_up = jnp.sum(grad_upward.astype(jnp.float32), axis=(0, 1))
    grad_normed_two = jnp.einsum(
        "btf,df->btd", grad_upward, up_weight, preferred_element_type=jnp.float32
    )
    unused, norm_back_two = jax.vjp(compressed_norm, residual, norm_gain_two)
    grad_residual, gain_second = norm_back_two(grad_normed_two)
    grad_residual = grad_residual + grad_output
    grad_residual_low = grad_residual.astype(jnp.bfloat16)
    grad_outward = jnp.einsum(
        "btf,btd->fd", attended_low, grad_residual_low, preferred_element_type=jnp.float32
    )
    bias_outward = jnp.sum(grad_residual_low.astype(jnp.float32), axis=(0, 1))
    grad_attended = (
        jnp.einsum(
            "btd,fd->btf", grad_residual_low, outward_weight, preferred_element_type=jnp.float32
        )
        .astype(jnp.bfloat16)
        .reshape(heads_shape)
    )
    delta_rows = jnp.sum(grad_attended.astype(jnp.float32) * attended, axis=-1)

    def backward_block(current, blocks, key_start):
        keys_block, values_block = (blocks[0], blocks[1])
        block_len = keys_block.shape[1]
        key_pos = key_start + jnp.arange(block_len, dtype=jnp.int32)
        allowed = block_masks(doc_lengths, query_pos, key_pos)
        query_grad = current[0]
        scores = (
            jnp.einsum(
                "bqhe,bkhe->bqhk", queries_low, keys_block, preferred_element_type=jnp.float32
            )
            * score_scale
        )
        scores = jnp.where(allowed, scores, FLOOR)
        weights = jnp.where(allowed, jnp.exp(scores - log_total[..., None]), 0.0)
        grad_weights = jnp.einsum(
            "bqhe,bkhe->bqhk", grad_attended, values_block, preferred_element_type=jnp.float32
        )
        grad_scores = (weights * (grad_weights - delta_rows[..., None])).astype(jnp.bfloat16)
        query_grad = (
            query_grad
            + jnp.einsum(
                "bqhk,bkhe->bqhe", grad_scores, keys_block, preferred_element_type=jnp.float32
            )
            * score_scale
        )
        key_grads = current[1]
        value_grads = current[2]
        value_part = jnp.einsum(
            "bqhk,bqhe->bkhe",
            weights.astype(jnp.bfloat16),
            grad_attended,
            preferred_element_type=jnp.float32,
        )
        key_part = (
            jnp.einsum(
                "bqhk,bqhe->bkhe", grad_scores, queries_low, preferred_element_type=jnp.float32
            )
            * score_scale
        )
        key_grads = lax.dynamic_update_slice_in_dim(
            key_grads,
            lax.dynamic_slice_in_dim(key_grads, key_start, block_len, 1) + key_part,
            key_start,
            1,
        )
        value_grads = lax.dynamic_update_slice_in_dim(
            value_grads,
            lax.dynamic_slice_in_dim(value_grads, key_start, block_len, 1) + value_part,
            key_start,
            1,
        )
        return (query_grad, key_grads, value_grads)

    row_len = local_len * lax.axis_size("seq")
    grads_shape = (batches, row_len, HEADS, HEAD_DIM)
    back_state = (
        jnp.zeros(heads_shape, jnp.float32),
        jnp.zeros(grads_shape, jnp.float32),
        jnp.zeros(grads_shape, jnp.float32),
    )
    folded = blockwise(
        backward_block,
        back_state,
        (
            lax.all_gather(keys_low, "seq", axis=1, tiled=True),
            lax.all_gather(values_low, "seq", axis=1, tiled=True),
        ),
    )
    query_grad = folded[0]
    key_mine, value_mine = (
        lax.psum_scatter(
            folded[1].astype(jnp.bfloat16), "seq", scatter_dimension=1, tiled=True
        ).astype(jnp.float32),
        lax.psum_scatter(
            folded[2].astype(jnp.bfloat16), "seq", scatter_dimension=1, tiled=True
        ).astype(jnp.float32),
    )
    flat_shape = (batches, local_len, head_width)
    grad_query_low = query_grad.reshape(flat_shape).astype(jnp.bfloat16)
    grad_key_low = key_mine.reshape(flat_shape).astype(jnp.bfloat16)
    grad_value_low = value_mine.reshape(flat_shape).astype(jnp.bfloat16)
    grad_projected = jnp.concatenate([grad_query_low, grad_key_low, grad_value_low], axis=-1)
    grad_inward = jnp.einsum(
        "btd,btf->df", normed_one, grad_projected, preferred_element_type=jnp.float32
    )
    bias_inward = jnp.stack(
        [
            jnp.sum(grad_query_low.astype(jnp.float32), axis=(0, 1)),
            jnp.sum(grad_value_low.astype(jnp.float32), axis=(0, 1)),
        ]
    )
    grad_normed_one = jnp.einsum(
        "btf,df->btd", grad_projected, inward_weight, preferred_element_type=jnp.float32
    )
    unused, norm_back_one = jax.vjp(compressed_norm, token_values, norm_gain_one)
    grad_first, gain_first = norm_back_one(grad_normed_one)
    grad_tokens = (grad_residual + grad_first).astype(jnp.bfloat16)
    small_sums = lax.psum(
        (gain_first, bias_inward, bias_outward, gain_second, bias_up, bias_down), ("seq", "dp")
    )
    matrices = (
        lax.psum_scatter(grad_inward, ("seq", "dp"), scatter_dimension=1, tiled=True),
        lax.psum_scatter(grad_outward, ("seq", "dp"), scatter_dimension=0, tiled=True),
        lax.psum_scatter(grad_up, ("seq", "dp"), scatter_dimension=1, tiled=True),
        lax.psum_scatter(grad_down, ("seq", "dp"), scatter_dimension=0, tiled=True),
    )
    return (
        output_tokens,
        grad_tokens,
        small_sums[0],
        matrices[0],
        small_sums[1],
        matrices[1],
        small_sums[2],
        small_sums[3],
        matrices[2],
        small_sums[4],
        matrices[3],
        small_sums[5],
    )


def solution(mesh):
    return jax.shard_map(
        local,
        mesh=mesh,
        in_specs=(
            P("dp", "seq", None),
            P("dp", None),
            P(),
            P(),
            P(),
            P(),
            P(),
            P(),
            P(),
            P(),
            P(),
            P(),
            P("dp", "seq", None),
        ),
        out_specs=(
            P("dp", "seq", None),
            P("dp", "seq", None),
            P(),
            P(None, ("seq", "dp")),
            P(),
            P(("seq", "dp"), None),
            P(),
            P(),
            P(None, ("seq", "dp")),
            P(),
            P(("seq", "dp"), None),
            P(),
        ),
        check_vma=False,
    )
```

profile of v0, /device:TPU:0, one launch (start us, length us, event | category | flops | bytes accessed | tf_op | source)
XLA Modules:
  0.0 770.1 jit_solution(354855084947024430)
XLA Ops:
  8.1 2.1 copy.110
  12.0 2.1 fusion.29
  16.4 1.9 copy.111
  18.4 2.4 fusion.73
  20.8 1.9 copy.113
  25.4 1.9 copy.116
  27.4 1.9 copy.112
  29.3 1.4 reduce_window_sum.16
  33.5 20.5 %all-gather.3.cloned.1.call-done = bf16[2,1024,12,64]{1,3,2,0:T(8,128)(2,1)} async-done(((bf16[2,128,12,64]{1,3,2,0:T(8,128)(2,1)}), bf16[2,1024,12,64]{1,3,2,0:T(8,128)(2,1)}) %all-gather.3.cloned.1.call-update) | async-done | bytes 3145744 | tf_op jit(solution)/shard_map/all_gather | solution.py:122
  54.0 4.9 fusion.5
  59.0 3.1 fusion.2
  64.3 24.4 %all-gather.5.cloned.1.call-done = bf16[2,1024,12,64]{1,3,2,0:T(8,128)(2,1)} async-done(((bf16[2,128,12,64]{1,3,2,0:T(8,128)(2,1)}), bf16[2,1024,12,64]{1,3,2,0:T(8,128)(2,1)}) %all-gather.5.cloned.1.call-update) | async-done | bytes 3145744 | tf_op jit(solution)/shard_map/all_gather | solution.py:123
  88.7 10.0 %fusion.90 = (bf16[2,128,12,64]{1,3,2,0:T(8,128)(2,1)S(1)}, f32[2,128,12,64]{1,3,2,0:T(8,128)}) fusion(f32[2,128,12]{1,2,0:T(8,128)} %get-tuple-element.167, bf16[2,1024,12,64]{1,3,2,0:T(8,128)(2,1)} %all-gather.5.cloned.1.call-done, f32[2,12,1024,128]{3,2,1,0:T(8,128)} %copy-done.1, f32[2,128,12]{1,2,0:T(8,128)} %copy-done.16, ...), kind=kOutput, calls=%fused_computation.125 | convolution fusion | flops 418971648 | bytes 17207296 | tf_op jit(solution)/shard_map/while/body/eval_jaxpr/bqhk,bkhe->bqhe/dot_general | solution.py:105
  99.5 1.5 fusion.24
  101.6 3.7 convert_reduce_fusion
  105.4 2.1 multiply_reduce_fusion
  110.6 1.9 copy.118
  113.9 8.6 %fusion.1 = bf16[2,128,12,1024]{1,3,2,0:T(8,128)(2,1)S(1)} fusion(f32[2,12,1024,128]{3,2,1,0:T(8,128)} %copy-done.1, f32[2,128,12]{1,2,0:T(8,128)S(1)} %multiply_reduce_fusion.1, f32[2,128,12]{1,2,0:T(8,128)} %get-tuple-element.166, pred[2,128,1024]{1,2,0:T(8,128)(4,1)} %compare_and_fusion, bf16[2,1024,12,64]{1,3,2,0:T(8,128)(2,1)} %all-gather.5.cloned.1.call-done, ...), kind=kOutput, calls=%fused_computation.2 | convolution fusion | flops 424673280 | bytes 22700032 | tf_op jit(solution)/shard_map/while/body/eval_jaxpr/bqhe,bkhe->bqhk/dot_general | solution.py:186
  122.5 2.7 copy-done.2
  125.1 3.9 fusion.38
  129.1 12.8 %copy.139 = bf16[2,1024,12,64]{3,2,0,1:T(8,128)(2,1)} copy(bf16[2,1024,12,64]{1,3,2,0:T(8,128)(2,1)} %fusion.38) | data formatting | bytes 6291456
  141.8 11.4 %reshape.192 = bf16[1024,1536]{1,0:T(8,128)(2,1)} reshape(bf16[1024,2,12,64]{3,2,1,0:T(8,128)(2,1)} %bitcast.118) | data formatting | bytes 6291456
  153.5 10.0 %convert_bitcast_fusion = bf16[2,1024,12,64]{1,3,2,0:T(8,128)(2,1)} fusion(bf16[2,128,12,64]{1,3,2,0:T(8,128)(2,1)} %bitcast.134, f32[2,12,1024,128]{3,2,1,0:T(8,128)} %copy-done.1, f32[2,128,12]{1,2,0:T(8,128)} %get-tuple-element.166, pred[2,128,1024]{1,2,0:T(8,128)(4,1)} %compare_and_fusion), kind=kOutput, calls=%fused_computation.46 | convolution fusion | flops 419954688 | bytes 16396288 | tf_op jit(solution)/shard_map/while/body/eval_jaxpr/bqhk,bqhe->bkhe/dot_general | solution.py:199
  163.6 12.8 %copy.141 = bf16[2,1024,12,64]{3,2,0,1:T(8,128)(2,1)} copy(bf16[2,1024,12,64]{1,3,2,0:T(8,128)(2,1)} %convert_bitcast_fusion) | data formatting | bytes 6291456
  176.4 11.5 %reshape.194 = bf16[1024,1536]{1,0:T(8,128)(2,1)} reshape(bf16[1024,2,12,64]{3,2,1,0:T(8,128)(2,1)} %bitcast.119) | data formatting | bytes 6291456
  187.9 3.1 convolution_bitcast_fusion.3
  191.1 8.0 %convolution_bitcast_fusion = f32[3072,767]{1,0:T(8,128)} fusion(bf16[2,128,767]{2,1,0:T(8,128)(2,1)} %copy.116, f32[2,128,3072]{2,1,0:T(8,128)} %copy-done.3), kind=kOutput, calls=%fused_computation.19 | convolution fusion | flops 1213464576 | bytes 12963328 | tf_op jit(solution)/shard_map/btf,btd->fd/dot_general | solution.py:143
  199.2 6.8 convolution_bitcast_fusion.1
  206.4 6.6 convert_reduce_fusion.5
  213.0 2.0 copy.122
  215.0 2.6 reshape.193
  217.6 2.8 copy.140
  220.3 1.9 copy.123
  222.3 27.3 %reduce-scatter.21.cloned.1.call-done = bf16[128,1536]{1,0:T(8,128)(2,1)} async-done(((bf16[1024,1536]{1,0:T(8,128)(2,1)}), bf16[128,1536]{1,0:T(8,128)(2,1)}) %reduce-scatter.21.cloned.1.call-update) | async-done | bytes 393232
  249.6 2.6 reshape.195
  252.1 2.8 copy.142
  254.9 1.9 copy.124
  256.8 5.4 convolution_bitcast_fusion.2
  262.9 6.3 fusion.55
  269.2 2.0 copy.129
  272.5 1.8 convert_reduce_fusion.4
  275.7 3.3 fusion.71
  280.1 2.0 copy.130
  282.8 41.1 %all-reduce = (f32[767]{0:T(1024)}, f32[2,768]{1,0:T(2,128)}, f32[767]{0:T(1024)}, f32[767]{0:T(1024)}, f32[3072]{0:T(1024)}, /*index=5*/f32[767]{0:T(1024)}) all-reduce(f32[767]{0:T(1024)} %get-tuple-element.143, f32[2,768]{1,0:T(2,128)S(1)} %pad_maximum_fusion.3, ...), channel_id=1, replica_groups=mesh['seq'=8,'dp'=4] {'seq','dp'}, use_global_device_ids=true, to_apply=%region_15.16 | all-reduce | flops 7676 | bytes 61408 | tf_op jit(solution)/shard_map/psum | solution.py:269
  323.9 30.4 %reduce-scatter.13.cloned.1.call-done = f32[24,767]{1,0:T(8,128)} async-done(((f32[768,767]{1,0:T(8,128)}), f32[24,767]{1,0:T(8,128)}) %reduce-scatter.13.cloned.1.call-update) | async-done | bytes 73648 | tf_op jit(solution)/shard_map/reduce_scatter | solution.py:274
  354.3 142.0 %reduce-scatter.17.cloned.1.call-done = f32[96,767]{1,0:T(8,128)} async-done(((f32[3072,767]{1,0:T(8,128)}), f32[96,767]{1,0:T(8,128)}) %reduce-scatter.17.cloned.1.call-update) | async-done | bytes 294544 | tf_op jit(solution)/shard_map/reduce_scatter | solution.py:276
  496.3 141.2 %reduce-scatter.15.cloned.1.call-done = f32[767,96]{0,1:T(8,128)} async-done(((f32[767,3072]{0,1:T(8,128)}), f32[767,96]{0,1:T(8,128)}) %reduce-scatter.15.cloned.1.call-update) | async-done | bytes 294544 | tf_op jit(solution)/shard_map/reduce_scatter | solution.py:275
  637.5 125.3 %reduce-scatter.11.cloned.1.call-done = f32[767,72]{0,1:T(8,128)} async-done(((f32[767,2304]{0,1:T(8,128)}), f32[767,72]{0,1:T(8,128)}) %reduce-scatter.11.cloned.1.call-update) | async-done | bytes 220912 | tf_op jit(solution)/shard_map/reduce_scatter | solution.py:273
  (103 shorter events, 24.4 us)
Async XLA Ops:
  7.2 4.8 copy-start
  7.2 46.8 %all-gather.3.cloned.1.call-start = ((), (), s32[]{:S(2)}) async-start(), calls=%async_computation.6 | async-start | bytes 3538944 | tf_op jit(solution)/shard_map/all_gather | solution.py:122
  11.4 0.6 copy-start.22
  11.4 2.7 copy-start.20
  12.0 6.4 copy-start.19
  14.2 1.4 copy-start.9
  18.3 70.4 %all-gather.5.cloned.1.call-start = ((), (), s32[]{:S(2)}) async-start(), calls=%async_computation.7 | async-start | bytes 3538944 | tf_op jit(solution)/shard_map/all_gather | solution.py:123
  22.7 192.3 %reduce-scatter.19.cloned.1.call-start = ((), (), s32[]{:S(2)}) async-start(), calls=%async_computation.12 | async-start | bytes 3538944
  54.0 5.0 copy-start.13
  58.9 4.6 copy-start.1
  58.9 4.7 copy-start.16
  88.7 10.7 %slice-start = ((s8[4718592]{0:T(1024)(128)(4,1)}), s8[4194304]{0:T(1024)(128)(4,1)S(1)}, s32[]{:S(2)}) async-start(s8[4718592]{0:T(1024)(128)(4,1)} %bitcast.120), calls=%async_computation.14 | async-start | bytes 8388608
  88.7 10.0 %copy-start.4 = (bf16[2,128,767]{2,1,0:T(8,128)(2,1)S(1)}, bf16[2,128,767]{2,1,0:T(8,128)(2,1)}, u32[]{:S(2)}) copy-start(bf16[2,128,767]{2,1,0:T(8,128)(2,1)} %copy.110) | copy-start | bytes 1178116
  88.7 10.0 %copy-start.10 = (bf16[768,767]{1,0:T(8,128)(2,1)S(1)}, bf16[768,767]{1,0:T(8,128)(2,1)}, u32[]{:S(2)}) copy-start(bf16[768,767]{1,0:T(8,128)(2,1)} %param.18) | copy-start | bytes 3534340
  88.7 10.7 %slice-start.1 = ((s8[4718592]{0:T(1024)(128)(4,1)}), s8[524288]{0:T(1024)(128)(4,1)S(1)}, s32[]{:S(2)}) async-start(s8[4718592]{0:T(1024)(128)(4,1)} %bitcast.120), calls=%async_computation.15 | async-start | bytes 1048576
  88.7 10.7 %copy-start.17 = (f32[3072]{0:T(1024)S(1)}, f32[3072]{0:T(1024)}, u32[]{:S(2)}) copy-start(f32[3072]{0:T(1024)} %convert_element_type.171) | copy-start | bytes 36868
  98.7 2.2 copy-start.14
  98.7 2.6 slice-start.2
  99.4 8.1 %copy-start.8 = (f32[2,128,767]{2,1,0:T(8,128)}, f32[2,128,767]{2,1,0:T(8,128)S(1)}, u32[]{:S(2)}) copy-start(f32[2,128,767]{2,1,0:T(8,128)S(1)} %get-tuple-element.173) | copy-start | bytes 2356228
  99.4 2.0 copy-start.11
  99.5 2.2 slice-start.3
  101.6 3.7 copy-start.3
  105.4 2.1 copy-start.15
  108.4 0.9 copy-start.6
  113.9 11.3 %copy-start.12 = (bf16[2,128,768]{1,2,0:T(8,128)(2,1)S(1)}, bf16[2,128,768]{1,2,0:T(8,128)(2,1)}, u32[]{:S(2)}) copy-start(bf16[2,128,768]{1,2,0:T(8,128)(2,1)} %copy.112) | copy-start | bytes 1179652
  122.5 2.7 copy-start.2
  153.3 96.3 %reduce-scatter.21.cloned.1.call-start = ((), (), s32[]{:S(2)}) async-start(), calls=%async_computation.13 | async-start | bytes 3538944
  187.9 166.5 %reduce-scatter.13.cloned.1.call-start = ((), (), s32[]{:S(2)}) async-start(), calls=%async_computation.9 | async-start | bytes 2433024 | tf_op jit(solution)/shard_map/reduce_scatter | solution.py:274
  191.1 305.2 %reduce-scatter.17.cloned.1.call-start = ((), (), s32[]{:S(2)}) async-start(), calls=%async_computation.11 | async-start | bytes 9732096 | tf_op jit(solution)/shard_map/reduce_scatter | solution.py:276
  199.2 438.3 %reduce-scatter.15.cloned.1.call-start = ((), (), s32[]{:S(2)}) async-start(), calls=%async_computation.10 | async-start | bytes 9732096 | tf_op jit(solution)/shard_map/reduce_scatter | solution.py:275
  206.1 556.8 %reduce-scatter.11.cloned.1.call-start = ((), (), s32[]{:S(2)}) async-start(), calls=%async_computation.8 | async-start | bytes 7299072 | tf_op jit(solution)/shard_map/reduce_scatter | solution.py:273
  262.2 0.7 copy-start.24
  275.6 3.3 copy-start.21
  275.6 3.3 copy-start.23
  275.6 3.3 copy-start.5
  275.7 3.4 copy-start.7
  279.0 3.8 copy-start.18
Sparse Core Ops, SparseCore 0:
  18.4 35.5 all-gather.2
  55.8 32.8 all-gather.4
  153.4 46.2 reduce-scatter.18
  203.3 46.2 reduce-scatter.20
  255.3 99.0 reduce-scatter.12
  361.6 134.5 reduce-scatter.16
  502.7 134.7 reduce-scatter.14
  644.7 118.0 reduce-scatter.10
where the time goes:
time: 781 us; the launch traced here: 770 us
  waiting for transfers between devices  511 us (65%)
  local copies, waits for them, and re-layouts  92.7 us (12%)
  matrix products  88.4 us (11%)
  blocking collectives  41.1 us (5%)
  other arithmetic  20.9 us (3%)
  between operations  14.9 us (2%)
    reduce_scatter x1, waiting for transfers between devices, local(): lax.psum_scatter(grad_down, ('seq', 'dp'), scatter_dimension=0, tiled=True)  142 us
    reduce_scatter x1, waiting for transfers between devices, local(): lax.psum_scatter(grad_up, ('seq', 'dp'), scatter_dimension=1, tiled=True)  141 us
    reduce_scatter x1, waiting for transfers between devices, local(): lax.psum_scatter(grad_inward, ('seq', 'dp'), scatter_dimension=1, tiled=T...  125 us
    unnamed x70, local copies, waits for them, and re-layouts  75.6 us
    psum x1, blocking collectives, local(): lax.psum((gain_first, bias_inward, bias_outward, gain_second, bias_up, bi...  41.1 us
    reduce_scatter x1, waiting for transfers between devices, local(): lax.psum_scatter(grad_outward, ('seq', 'dp'), scatter_dimension=0, tiled=...  30.4 us
    unnamed x10, waiting for transfers between devices  27.4 us
    all_gather x1, waiting for transfers between devices, local(): lax.all_gather(values_low, 'seq', axis=1, tiled=True)  24.4 us
  transfers between devices with their start and end apart: 8, of which 7 were waited for; matrix products, arithmetic and copies ran while one was open for 16% of the time, Pallas kernels for 0%

commit v1 on v0

v1 whole, which is shorter than its diff:
```python
import functools

import jax
import jax.numpy as jnp
from jax import lax
from jax.experimental import pallas as pl
from jax.experimental.pallas import tpu as pltpu
from jax.sharding import PartitionSpec as P

HEADS = 12
HEAD_DIM = 64
EPSILON = 1e-05
FLOOR = -1e30
QB = 256
F32 = jnp.float32
BF16 = jnp.bfloat16


def inverse_rms(values):
    squares = jnp.sum(values * values, axis=-1, keepdims=True)
    totals = jnp.sum(values, axis=-1, keepdims=True)
    return lax.rsqrt((squares + totals * totals) / (values.shape[-1] + 1) + EPSILON), totals


def norm_back(values, gain, inverse, totals, incoming):
    weighted = incoming * gain
    dots = jnp.sum(weighted * values, axis=-1, keepdims=True)
    factor = inverse * inverse * inverse * dots / (values.shape[-1] + 1)
    grad = inverse * weighted - factor * (values + totals)
    return grad, jnp.sum(incoming * values * inverse, axis=0)


def dot(left, right, left_dim, right_dim):
    return lax.dot_general(
        left, right, (((left_dim,), (right_dim,)), ((), ())), preferred_element_type=F32
    )


def allowed_block(ends, query_start, keys):
    query_pos = query_start + lax.broadcasted_iota(jnp.int32, (QB, 1), 0)
    start = jnp.zeros_like(query_pos)
    for end in ends:
        start = jnp.where(query_pos >= end, end, start)
    key_pos = lax.broadcasted_iota(jnp.int32, (1, keys), 1)
    return (key_pos <= query_pos) & (key_pos >= start)


def attention_forward(heads, length, ends_ref, qkv_ref, attended_ref, log_ref):
    width = heads * HEAD_DIM
    ends = [ends_ref[at] for at in range(3)]
    for block in range(length // QB):
        rows = pl.ds(block * QB, QB)
        keys = (block + 1) * QB
        allowed = allowed_block(ends, block * QB, keys)
        for head in range(heads):
            at = head * HEAD_DIM
            query = qkv_ref[rows, at : at + HEAD_DIM] * BF16(HEAD_DIM**-0.5)
            key = qkv_ref[:keys, width + at : width + at + HEAD_DIM]
            value = qkv_ref[:keys, 2 * width + at : 2 * width + at + HEAD_DIM]
            scores = jnp.where(allowed, dot(query, key, 1, 1), FLOOR)
            top = jnp.max(scores, axis=-1, keepdims=True)
            weights = jnp.exp(scores - top)
            total = jnp.sum(weights, axis=-1, keepdims=True)
            attended = dot(weights.astype(BF16), value, 1, 0) / total
            attended_ref[rows, at : at + HEAD_DIM] = attended
            log_ref[rows, head : head + 1] = top + jnp.log(total)


def attention_backward(
    heads, length, ends_ref, qkv_ref, attended_ref, log_ref, grad_ref, out_ref, key_grad, value_grad
):
    width = heads * HEAD_DIM
    ends = [ends_ref[at] for at in range(3)]
    blocks = length // QB
    for head in range(heads):
        at = head * HEAD_DIM
        for block in reversed(range(blocks)):
            rows = pl.ds(block * QB, QB)
            keys = (block + 1) * QB
            allowed = allowed_block(ends, block * QB, keys)
            query = qkv_ref[rows, at : at + HEAD_DIM] * BF16(HEAD_DIM**-0.5)
            key = qkv_ref[:keys, width + at : width + at + HEAD_DIM]
            value = qkv_ref[:keys, 2 * width + at : 2 * width + at + HEAD_DIM]
            grad = grad_ref[rows, at : at + HEAD_DIM]
            delta = jnp.sum(
                grad.astype(F32) * attended_ref[rows, at : at + HEAD_DIM], axis=-1, keepdims=True
            )
            scores = dot(query, key, 1, 1)
            weights = jnp.where(allowed, jnp.exp(scores - log_ref[rows, head : head + 1]), 0.0)
            grad_weights = dot(grad, value, 1, 1)
            grad_scores = (weights * (grad_weights - delta)).astype(BF16)
            out_ref[rows, at : at + HEAD_DIM] = (
                dot(grad_scores, key, 1, 0) * HEAD_DIM**-0.5
            ).astype(BF16)
            key_part = dot(grad_scores, query, 0, 0)
            value_part = dot(weights.astype(BF16), grad, 0, 0)
            if block == blocks - 1:
                key_grad[...] = key_part
                value_grad[...] = value_part
            else:
                key_grad[:keys, :] += key_part
                value_grad[:keys, :] += value_part
        out_ref[:, width + at : width + at + HEAD_DIM] = key_grad[...].astype(BF16)
        out_ref[:, 2 * width + at : 2 * width + at + HEAD_DIM] = value_grad[...].astype(BF16)


def flip(value, mask, axis="seq"):
    return lax.ppermute(value, axis, [(at, at ^ mask) for at in range(lax.axis_size(axis))])


def pick(value, index, axis):
    return lax.dynamic_index_in_dim(value, index, axis, keepdims=False)


def halving(value, stages):
    kept = value
    for axis, mask, at, bit in stages:
        sent = pick(kept, 1 - bit, at).astype(BF16)
        kept = pick(kept, bit, at).astype(F32) + flip(sent, mask, axis).astype(F32)
    return kept


def bits_of(size):
    return [1 << at for at in range(size.bit_length() - 1)]


def local(
    tokens, doc_lengths, first_gain, inward_weight, inward_bias, outward_weight, outward_bias,
    second_gain, up_weight, up_bias, down_weight, down_bias, cotangent,
):
    rows, local_len, width = tokens.shape
    seq, dp = lax.axis_size("seq"), lax.axis_size("dp")
    me, replica = lax.axis_index("seq"), lax.axis_index("dp")
    core, chip, chips = me % 2, me // 2, seq // 2
    block = rows * local_len
    length = seq * local_len
    head_width = HEADS * HEAD_DIM
    heads = -(-HEADS // chips)
    mine = heads * HEAD_DIM
    slots = chips * mine
    order = jnp.arange(chips, dtype=jnp.int32) ^ chip

    def to_rows(value):
        kept, got = pick(value, core, 0), flip(pick(value, 1 - core, 0), 1)
        first, second = jnp.where(core == 0, kept, got), jnp.where(core == 0, got, kept)
        return jnp.concatenate([first, second], axis=0)

    def from_rows(value):
        halves = value.reshape(2, local_len, width)
        kept, got = pick(halves, core, 0), flip(pick(halves, 1 - core, 0), 1)
        return jnp.where(core == 0, jnp.stack([kept, got]), jnp.stack([got, kept]))

    def gather_chips(value):
        if chips == 4:
            half = value.shape[0] // 2
            one, two = flip(value, 2), flip(value, 4)
            three = jnp.concatenate([flip(two[:half], 2), flip(one[half:], 4)], axis=0)
            return jnp.stack([value, one, two, three])
        held = value[None]
        for bit in bits_of(chips):
            held = jnp.concatenate([held, flip(held, 2 * bit)], axis=0)
        return held

    def exchange(pieces):
        return [pieces[0]] + [flip(pieces[at], 2 * at) for at in range(1, chips)]

    mine_rows = to_rows(tokens)
    row_tokens = jnp.take(gather_chips(mine_rows), order, axis=0).reshape(length, width)
    cot_rows = to_rows(cotangent)
    token_values = mine_rows.astype(F32)
    cot_values = cot_rows.astype(F32)
    gain_one, gain_two = first_gain.astype(F32), second_gain.astype(F32)

    inward_t = inward_weight.T.reshape(3, head_width, width)
    outward_p = outward_weight
    bias_q, bias_v = inward_bias[0], inward_bias[1]
    if slots != head_width:
        inward_t = jnp.pad(inward_t, ((0, 0), (0, slots - head_width), (0, 0)))
        outward_p = jnp.pad(outward_p, ((0, slots - head_width), (0, 0)))
        bias_q = jnp.pad(bias_q, (0, slots - head_width))
        bias_v = jnp.pad(bias_v, (0, slots - head_width))
    inward_x = jnp.take(inward_t.reshape(3, chips, mine, width), order, axis=1)
    inward_x = inward_x.transpose(1, 0, 2, 3).reshape(chips, 3 * mine, width)
    outward_x = jnp.take(outward_p.reshape(chips, mine, width), order, axis=0).reshape(slots, width)
    bias_mine = jnp.concatenate(
        [pick(bias_q.reshape(chips, mine), chip, 0), jnp.zeros((mine,), BF16), pick(bias_v.reshape(chips, mine), chip, 0)]
    )

    row_values = row_tokens.astype(F32)
    row_inverse, unused = inverse_rms(row_values)
    row_normed = (row_values * gain_one * row_inverse).astype(BF16)
    qkv = (dot(row_normed, inward_x[0], 1, 1) + bias_mine.astype(F32)).astype(BF16)
    ends = jnp.cumsum(pick(doc_lengths, core, 0))[:3]
    whole = pl.BlockSpec(memory_space=pltpu.VMEM)
    scalars = pl.BlockSpec(memory_space=pltpu.SMEM)
    params = pltpu.CompilerParams(vmem_limit_bytes=48 * 1024 * 1024)
    attended, log_total = pl.pallas_call(
        functools.partial(attention_forward, heads, length),
        out_shape=(
            jax.ShapeDtypeStruct((length, mine), F32),
            jax.ShapeDtypeStruct((length, 8), F32),
        ),
        in_specs=[scalars, whole],
        out_specs=(whole, whole),
        compiler_params=params,
        cost_estimate=pl.CostEstimate(flops=8 * length * length * mine, bytes_accessed=8 * length * mine, transcendentals=0),
        name="attention_forward",
    )(ends, qkv)
    attended_blocks = jnp.take(attended.astype(BF16).reshape(chips, block, mine), order, axis=0)
    attended_low = jnp.concatenate(exchange(attended_blocks), axis=-1)

    residual = token_values + (dot(attended_low, outward_x, 1, 0) + outward_bias.astype(F32))
    inverse_two, totals_two = inverse_rms(residual)
    normed_two = (residual * gain_two * inverse_two).astype(BF16)
    upward = dot(normed_two, up_weight, 1, 0) + up_bias.astype(F32)
    grad_active = dot(cot_rows, down_weight, 1, 1)
    active, gelu_back = jax.vjp(jax.nn.gelu, upward)
    active_low = active.astype(BF16)
    grad_upward = gelu_back(grad_active)[0].astype(BF16)
    grad_normed_two = dot(grad_upward, up_weight, 1, 1)
    grad_inner, gain_second = norm_back(residual, gain_two, inverse_two, totals_two, grad_normed_two)
    grad_residual = cot_values + grad_inner
    grad_low = grad_residual.astype(BF16)
    grad_attended = dot(grad_low, outward_x, 1, 1).astype(BF16).reshape(block, chips, mine)
    output_rows = residual + (dot(active_low, down_weight, 1, 0) + down_bias.astype(F32))
    output_tokens = from_rows(output_rows.astype(BF16))

    grad_row = exchange([grad_attended[:, at] for at in range(chips)])
    grad_row = jnp.take(jnp.stack(grad_row), order, axis=0).reshape(length, mine)
    grad_qkv = pl.pallas_call(
        functools.partial(attention_backward, heads, length),
        out_shape=jax.ShapeDtypeStruct((length, 3 * mine), BF16),
        in_specs=[scalars, whole, whole, whole, whole],
        out_specs=whole,
        scratch_shapes=[pltpu.VMEM((length, HEAD_DIM), F32)] * 2,
        compiler_params=params,
        cost_estimate=pl.CostEstimate(flops=20 * length * length * mine, bytes_accessed=16 * length * mine, transcendentals=0),
        name="attention_backward",
    )(ends, qkv, attended, log_total, grad_row)
    grad_blocks = jnp.take(grad_qkv.reshape(chips, block, 3 * mine), order, axis=0)
    grad_projected = jnp.concatenate(exchange(grad_blocks), axis=-1)
    grad_normed_one = dot(grad_projected, inward_x.reshape(chips * 3 * mine, width), 1, 0)
    inverse_one, totals_one = inverse_rms(token_values)
    normed_one = (token_values * gain_one * inverse_one).astype(BF16)
    grad_first, gain_first = norm_back(token_values, gain_one, inverse_one, totals_one, grad_normed_one)
    grad_tokens = from_rows((grad_residual + grad_first).astype(BF16))

    def chip_pair(value):
        return jnp.concatenate([value, flip(value, 1)], axis=0)

    def halves(value):
        parts = value.reshape(block, chips, 2, -1)
        return jnp.concatenate(
            [pick(parts, core, 2).reshape(block, -1), flip(pick(parts, 1 - core, 2).reshape(block, -1), 1)], axis=0
        )

    chip_bits, dp_bits = bits_of(chips), bits_of(dp)
    plane_shape = (2,) * len(chip_bits)
    dp_shape = (2,) * len(dp_bits)

    def stages(bits_in_order, with_core):
        axes = [("seq", 2 * bit) for bit in reversed(chip_bits)]
        if with_core:
            axes.append(("seq", 1))
        axes += [("dp", bit) for bit in reversed(dp_bits)]
        out = []
        for axis, mask in bits_in_order:
            at = axes.index((axis, mask))
            axes.pop(at)
            index = me if axis == "seq" else replica
            out.append((axis, mask, at, (index & mask) // mask))
        return out

    xs = [("seq", 2 * bit) for bit in chip_bits]
    zs = [("dp", bit) for bit in dp_bits]
    ff = up_weight.shape[1]
    ff_share = ff // (seq * dp)
    plane = plane_shape + dp_shape
    grad_down = dot(halves(active_low), chip_pair(cot_rows), 0, 0).reshape(plane + (ff_share, width))
    grad_up = dot(halves(grad_upward), chip_pair(normed_two), 0, 0).reshape(plane + (ff_share, width))
    down_share = halving(grad_down, stages(xs + zs, False))
    up_share = halving(grad_up, stages(xs[::-1] + zs, False))

    grad_in = dot(grad_projected, normed_one, 0, 0).reshape(chips, 3, mine, width)
    grad_in = jnp.take(grad_in, order, axis=0).transpose(1, 0, 2, 3).reshape(3, slots, width)
    grad_in = grad_in[:, :head_width].reshape(plane_shape + (2,) + dp_shape + (-1, width))
    grad_out = dot(attended_low, grad_low, 0, 0).reshape(chips, mine, width)
    grad_out = jnp.take(grad_out, order, axis=0).reshape(slots, width)[:head_width]
    grad_out = grad_out.reshape(plane_shape + (2,) + dp_shape + (-1, width))
    both = jnp.concatenate([grad_in, grad_out], axis=-2)
    in_share = grad_in.shape[-2]
    cut = both.shape[-2] // 2
    first = halving(both[..., :cut, :], stages([("seq", 1)] + xs + zs, True))
    second = halving(both[..., cut:, :], stages([("seq", 1)] + xs[::-1] + zs, True))
    shares = jnp.concatenate([first, second], axis=0)

    grad_p = grad_projected.reshape(block, chips, 3, mine).astype(F32).sum(axis=0)
    grad_p = jnp.take(grad_p, order, axis=0).transpose(1, 0, 2).reshape(3, slots)[:, :head_width]
    small = [
        gain_first, grad_p[0], grad_p[2], jnp.sum(grad_low.astype(F32), axis=0), gain_second,
        jnp.sum(grad_upward.astype(F32), axis=0), jnp.sum(cot_values, axis=0),
    ]
    sizes = [member.shape[0] for member in small]
    vector = jnp.concatenate(small)
    vector = jnp.pad(vector, (0, -vector.shape[0] % 1024)).reshape(-1, 128)
    for axis, mask in [("seq", 1)] + xs + zs:
        vector = vector + flip(vector, mask, axis)
    vector = vector.reshape(-1)
    sums, at = [], 0
    for size in sizes:
        sums.append(vector[at : at + size])
        at += size

    return (
        output_tokens,
        grad_tokens,
        sums[0],
        shares[:in_share].T,
        jnp.stack([sums[1], sums[2]]),
        shares[in_share:],
        sums[3],
        sums[4],
        up_share.T,
        sums[5],
        down_share,
        sums[6],
    )


def solution(mesh):
    return jax.shard_map(
        local,
        mesh=mesh,
        in_specs=(P("dp", "seq", None), P("dp", None)) + (P(),) * 10 + (P("dp", "seq", None),),
        out_specs=(
            P("dp", "seq", None),
            P("dp", "seq", None),
            P(),
            P(None, ("seq", "dp")),
            P(),
            P(("seq", "dp"), None),
            P(),
            P(),
            P(None, ("seq", "dp")),
            P(),
            P(("seq", "dp"), None),
            P(),
        ),
        check_vma=False,
    )
```

time: 781 us -> 340 us (0.44)
  waiting for transfers between devices: 511 us -> 91.2 us
  starting transfers between devices: 0.8 us -> 51.2 us
  matrix products: 88.4 us -> 41.8 us
  blocking collectives: 41.1 us -> 0 us
  Pallas kernels: 0 us -> 14.2 us
  between operations: 14.9 us -> 2.3 us
  other arithmetic: 20.9 us -> 32.7 us
  local copies, waits for them, and re-layouts: 92.7 us -> 103 us
    reduce_scatter x4 -> x0, waiting for transfers between devices: 439 us -> none  [the longest x1 142 us: local(): lax.psum_scatter(grad_down, ('seq', 'dp'), scatter_dimension=0, tiled=True)]
    ppermute x0 -> x44, waiting for transfers between devices: none -> 91.2 us  [flip(): lax.ppermute(value, axis, [(at, at ^ mask) for at in range(lax.axis_size(...]
    ppermute x0 -> x44, starting transfers between devices: none -> 51.2 us  [flip(): lax.ppermute(value, axis, [(at, at ^ mask) for at in range(lax.axis_size(...]
    dot_general x18 -> x12, matrix products: 88.4 us -> 41.8 us  [dot(): lax.dot_general(left, right, (((left_dim,), (right_dim,)), ((), ())), pre...]
    all_gather x2 -> x0, waiting for transfers between devices: 44.9 us -> none  [the longest x1 24.4 us: local(): lax.all_gather(values_low, 'seq', axis=1, tiled=True)]
    unnamed x70 -> x151, local copies, waits for them, and re-layouts: 75.6 us -> 31.9 us
    psum x1 -> x0, blocking collectives: 41.1 us -> none  [local(): lax.psum((gain_first, bias_inward, bias_outward, gain_second, bias_up, bi...]
    unnamed x10 -> x0, waiting for transfers between devices: 27.4 us -> none
  transfers between devices with their start and end apart: 8 -> 44, of which waited for: 7 -> 19; matrix products, arithmetic and copies ran while one was open for 16% -> 49% of each run, Pallas kernels for 0% -> 4%
where the time goes in v1:
time: 340 us; the launch traced here: 336 us
  local copies, waits for them, and re-layouts  103 us (30%)
  waiting for transfers between devices  91.2 us (27%)
  starting transfers between devices  51.2 us (15%)
  matrix products  41.8 us (12%)
  other arithmetic  32.7 us (10%)
  Pallas kernels  14.2 us (4%)
    ppermute x44, waiting for transfers between devices, flip(): lax.ppermute(value, axis, [(at, at ^ mask) for at in range(lax.axis_size(...  91.2 us
    ppermute x44, starting transfers between devices, flip(): lax.ppermute(value, axis, [(at, at ^ mask) for at in range(lax.axis_size(...  51.2 us
    dot_general x12, matrix products, dot(): lax.dot_general(left, right, (((left_dim,), (right_dim,)), ((), ())), pre...  41.8 us
    unnamed x151, local copies, waits for them, and re-layouts  31.9 us
    dynamic_slice x11, local copies, waits for them, and re-layouts, pick(): return lax.dynamic_index_in_dim(value, index, axis, keepdims=False)  19.4 us
    reshape x2, local copies, waits for them, and re-layouts, halves(): parts = value.reshape(block, chips, 2, -1)  9.48 us
    pallas_call x1, Pallas kernels, local(): pl.pallas_call(functools.partial(attention_backward, heads, length), out_...  8.55 us
    gather x1, local copies, waits for them, and re-layouts, local(): jnp.take(grad_in, order, axis=0).transpose(1, 0, 2, 3)  7.06 us
  transfers between devices with their start and end apart: 44, of which 19 were waited for; matrix products, arithmetic and copies ran while one was open for 49% of the time, Pallas kernels for 4%

profile of v1, /device:TPU:0, one launch (start us, length us, event | category | flops | bytes accessed | tf_op | source)
XLA Modules:
  0.0 336.2 jit_solution(10512844311551587650)
XLA Ops:
  0.8 2.0 constant_dynamic-slice_fusion.18
  10.7 6.0 %copy.64 = bf16[767,2304]{0,1:T(8,128)(2,1)} copy(bf16[767,2304]{1,0:T(8,128)(2,1)} %param.18) | data formatting | bytes 7068672 | tf_op args[3]
  16.7 4.0 %copy.65 = bf16[3,4,192,767]{3,2,0,1:T(8,128)(2,1)} copy(bf16[3,4,192,767]{3,2,1,0:T(8,128)(2,1)} %bitcast.199) | data formatting | bytes 7068672 | tf_op jit(solution)/shard_map/reshape;reshape | solution.py:182
  21.3 4.6 %gather_fusion.1 = bf16[4,3,192,767]{3,2,1,0:T(8,128)(2,1)} fusion(bf16[3,4,192,767]{3,2,0,1:T(8,128)(2,1)} %copy.65, s32[1024]{0:T(1024)S(1)} %pad_clamp_fusion.1), kind=kCustom, calls=%fused_computation.3 | custom fusion | bytes 7068688 | tf_op jit(solution)/shard_map/jit(_take)/gather | solution.py:182
  25.9 2.4 broadcast_select_fusion
  32.5 3.0 collective-permute-start.2
  37.6 7.3 %collective-permute-done.2 = bf16[256,767]{1,0:T(8,128)(2,1)S(1)} collective-permute-done((bf16[256,767]{1,0:T(8,128)(2,1)S(1)}, bf16[256,767]{1,0:T(8,128)(2,1)S(1)}, u32[]{:S(2)}, u32[]{:S(2)}) %collective-permute-start.2) | collective-permute-done | bytes 392736 | tf_op jit(solution)/shard_map/ppermute | solution.py:108
  54.0 2.1 gather_fusion
  58.8 5.7 %attention_forward.1 = (f32[1024,192]{1,0:T(8,128)S(1)}, f32[1024,8]{1,0:T(8,128)S(1)}) custom-call(s32[3]{0:T(128)S(1)} %slice_bitcast_fusion.11.ends_ref, bf16[1024,576]{1,0:T(8,128)(2,1)S(1)} %add_convert_fusion.qkv_ref), custom_call_target="tpu_custom_call" | custom-call | flops 1610612736 | bytes 1572864 | tf_op jit(solution)/shard_map/attention_forward/pallas_call | solution.py:197
  68.9 2.6 collective-permute-done.7
  73.0 2.0 fusion.89
  75.9 6.8 %multiply_convert_fusion = (bf16[256,3072]{1,0:T(8,128)(2,1)}, f32[256,3072]{1,0:T(8,128)S(1)}) fusion(f32[3072]{0:T(1024)S(1)} %copy-done.51, bf16[256,767]{1,0:T(8,128)(2,1)} %multiply_convert_fusion.1, bf16[767,3072]{1,0:T(8,128)(2,1)} %param.23), kind=kOutput, calls=%fused_computation.32 | convolution fusion | flops 1214251008 | bytes 9836032 | tf_op jit(solution)/shard_map/dot_general | solution.py:34
  82.7 4.7 %convert_reduce_fusion.1 = (f32[3072]{0:T(1024)}, bf16[256,3072]{1,0:T(8,128)(2,1)S(1)}) fusion(f32[256,3072]{1,0:T(8,128)S(1)} %get-tuple-element.97, bf16[3072,767]{1,0:T(8,128)(2,1)S(1)} %bitcast.227, bf16[128,767]{1,0:T(8,128)(2,1)S(1)} %copy-done.23, bf16[128,767]{1,0:T(8,128)(2,1)S(1)} %get-tuple-element.77), kind=kOutput, calls=%fused_computation.31 | convolution fusion | flops 1224470528 | bytes 9836032 | tf_op jit(solution)/shard_map/dot_general | solution.py:34
  88.6 3.0 multiply_reduce_fusion
  91.6 5.0 %reshape.352 = bf16[256,4,2,384]{3,2,1,0:T(2,128)(2,1)} reshape(bf16[256,3072]{1,0:T(8,128)(2,1)} %copy-done.26) | data formatting | bytes 3145728 | tf_op jit(solution)/shard_map/reshape | solution.py:252
  96.6 4.5 %reshape.356 = bf16[256,4,2,384]{3,2,1,0:T(2,128)(2,1)S(1)} reshape(bf16[256,3072]{1,0:T(8,128)(2,1)} %get-tuple-element.96) | data formatting | bytes 3145728 | tf_op jit(solution)/shard_map/reshape | solution.py:252
  101.2 4.5 %fusion.25 = bf16[256,767]{1,0:T(8,128)(2,1)S(1)} fusion(f32[256,767]{1,0:T(8,128)} %copy-done.18, bf16[256,3072]{1,0:T(8,128)(2,1)} %get-tuple-element.96, bf16[3072,767]{1,0:T(8,128)(2,1)} %param.25, f32[767]{0:T(1024)S(1)} %copy-done.55), kind=kOutput, calls=%fused_computation.67 | convolution fusion | flops 1206975744 | bytes 7466492 | tf_op jit(solution)/shard_map/dot_general | solution.py:34
  109.6 1.9 copy.69
  113.3 1.9 collective-permute-start.12
  116.9 6.8 %constant_dynamic-slice_fusion.7 = (bf16[256,4,1,384]{3,2,1,0:T(2,128)(2,1)}, bf16[256,4,1,384]{3,2,1,0:T(2,128)(2,1)}) fusion(bf16[256,4,2,384]{3,2,1,0:T(2,128)(2,1)} %reshape.352, s32[]{:T(128)S(6)} %select_n.251, s32[]{:T(128)S(6)} %select_n.252), kind=kLoop, calls=%fused_computation.187 | loop fusion | bytes 3145736 | tf_op jit(solution)/shard_map/jit(dynamic_index_in_dim)/dynamic_slice | solution.py:112
  123.7 2.1 fusion.69
  125.9 4.9 %constant_dynamic-slice_fusion.3 = (bf16[256,4,1,384]{3,2,1,0:T(2,128)(2,1)}, bf16[256,4,1,384]{3,2,1,0:T(2,128)(2,1)}) fusion(bf16[256,4,2,384]{3,2,1,0:T(2,128)(2,1)S(1)} %reshape.356, s32[]{:T(128)S(6)} %select_n.251, s32[]{:T(128)S(6)} %select_n.252), kind=kLoop, calls=%fused_computation.183 | loop fusion | bytes 3145736 | tf_op jit(solution)/shard_map/jit(dynamic_index_in_dim)/dynamic_slice | solution.py:112
  130.7 3.9 %gather_fusion.6 = f32[4,192,767]{2,1,0:T(8,128)} fusion(f32[4,192,767]{2,1,0:T(8,128)} %bitcast.201, s32[1024]{0:T(1024)} %copy-done.50), kind=kCustom, calls=%fused_computation.8 | custom fusion | bytes 4712464 | tf_op jit(solution)/shard_map/jit(_take)/gather | solution.py:288
  134.7 4.8 %copy.88 = bf16[256,4,1,384]{0,3,1,2:T(8,128)(2,1)} copy(bf16[256,4,1,384]{3,2,1,0:T(2,128)(2,1)} %get-tuple-element.59) | data formatting | bytes 1572864
  139.4 3.2 copy.89
  142.6 4.7 %copy.91 = bf16[256,4,1,384]{0,3,1,2:T(8,128)(2,1)} copy(bf16[256,4,1,384]{3,2,1,0:T(2,128)(2,1)} %get-tuple-element.57) | data formatting | bytes 1572864
  147.4 3.4 copy.92
  154.0 8.5 %attention_backward.1 = bf16[1024,576]{1,0:T(8,128)(2,1)S(1)} custom-call(s32[3]{0:T(128)S(1)} %slice_bitcast_fusion.11.ends_ref, bf16[1024,576]{1,0:T(8,128)(2,1)S(1)} %copy-done.3, f32[1024,192]{1,0:T(8,128)S(1)} %get-tuple-element.15.attended_ref, f32[1024,8]{1,0:T(8,128)S(1)} %get-tuple-element.16.log_ref, bf16[1024,192]{1,0:T(8,128)(2,1)S(1)} %bitcast.190), custom_call_target="tpu_custom_call" | custom-call | flops 4026531840 | bytes 3145728 | tf_op jit(solution)/shard_map/attention_backward/pallas_call | solution.py:230
  165.3 1.9 collective-permute-start.15
  172.1 4.2 %collective-permute-done.15 = bf16[256,576]{0,1:T(8,128)(2,1)S(1)} collective-permute-done((bf16[256,576]{0,1:T(8,128)(2,1)}, bf16[256,576]{0,1:T(8,128)(2,1)S(1)}, u32[]{:S(2)}, u32[]{:S(2)}) %collective-permute-start.15) | collective-permute-done | bytes 294944 | tf_op jit(solution)/shard_map/ppermute | solution.py:108
  176.3 5.0 %collective-permute-done.14 = bf16[256,576]{0,1:T(8,128)(2,1)} collective-permute-done((bf16[256,576]{0,1:T(8,128)(2,1)}, bf16[256,576]{0,1:T(8,128)(2,1)}, u32[]{:S(2)}, u32[]{:S(2)}) %collective-permute-start.14) | collective-permute-done | bytes 294944 | tf_op jit(solution)/shard_map/ppermute | solution.py:108
  185.1 5.1 %fusion.37 = (f32[767]{0:T(1024)}, f32[256]{0:T(256)S(1)}, f32[256,767]{1,0:T(8,128)}) fusion(f32[256]{0:T(256)S(1)} %add_rsqrt_fusion.1, bf16[128,767]{1,0:T(8,128)(2,1)S(1)} %copy-done.16, bf16[128,767]{1,0:T(8,128)(2,1)S(1)} %copy-done.14, f32[767]{0:T(1024)S(1)} %convert_element_type.257, bf16[2304,767]{1,0:T(8,128)(2,1)} %bitcast.202, ...), kind=kOutput, calls=%fused_computation.94 | convolution fusion | flops 911471104 | bytes 5900280 | tf_op jit(solution)/shard_map/dot_general | solution.py:34
  199.0 5.1 %fusion.52 = f32[2304,767]{1,0:T(8,128)} fusion(f32[767]{0:T(1024)S(1)} %convert_element_type.257, f32[256]{0:T(256)S(1)} %add_rsqrt_fusion.1, bf16[256,576]{0,1:T(8,128)(2,1)S(1)} %copy-done.30, bf16[256,576]{0,1:T(8,128)(2,1)} %collective-permute-done.14, bf16[256,576]{0,1:T(8,128)(2,1)} %collective-permute-done.13, bf16[256,576]{0,1:T(8,128)(2,1)S(1)} %copy-done.28, ...), kind=kOutput, calls=%fused_computation.123 | convolution fusion | flops 910883072 | bytes 8645116 | tf_op jit(solution)/shard_map/dot_general | solution.py:34
  204.1 7.1 %gather_fusion.5 = f32[4,3,192,767]{3,2,1,0:T(8,128)} fusion(f32[4,3,192,767]{3,2,1,0:T(8,128)} %bitcast.196, s32[1024]{0:T(1024)} %copy-done.50), kind=kCustom, calls=%fused_computation.7 | custom fusion | bytes 14137360 | tf_op jit(solution)/shard_map/jit(_take)/gather | solution.py:285
  212.3 3.7 %select_bitcast_fusion = f32[3,4,192,767]{3,2,0,1:T(8,128)S(1)} fusion(f32[4,3,192,767]{3,2,1,0:T(8,128)} %gather_fusion.5, pred[4]{0:T(512)(128)(4,1)S(1)} %compare_and_fusion), kind=kLoop, calls=%fused_computation.9 | loop fusion | flops 1767168 | bytes 14137348 | tf_op jit(solution)/shard_map/jit(_take)/select_n | solution.py:285
  221.1 2.7 collective-permute-start.21
  231.7 2.9 fusion.20
  235.9 3.0 fusion.16
  244.3 19.3 %collective-permute-done.40 = bf16[2,2,2,96,767]{4,3,1,2,0:T(8,128)(2,1)S(1)} collective-permute-done((bf16[2,2,2,96,767]{4,3,1,2,0:T(8,128)(2,1)S(1)}, bf16[2,2,2,96,767]{4,3,1,2,0:T(8,128)(2,1)S(1)}, u32[]{:S(2)}, u32[]{:S(2)}) %collective-permute-start.40) | collective-permute-done | bytes 1178144 | tf_op jit(solution)/shard_map/ppermute | solution.py:108
  265.0 2.9 collective-permute-done.34
  269.3 11.2 %collective-permute-done.28 = bf16[2,2,2,48,767]{4,3,2,1,0:T(8,128)(2,1)S(1)} collective-permute-done((bf16[2,2,2,48,767]{4,3,2,1,0:T(8,128)(2,1)S(1)}, bf16[2,2,2,48,767]{4,3,2,1,0:T(8,128)(2,1)S(1)}, u32[]{:S(2)}, u32[]{:S(2)}) %collective-permute-start.28) | collective-permute-done | bytes 589088 | tf_op jit(solution)/shard_map/ppermute | solution.py:108
  283.0 11.4 %collective-permute-done.29 = bf16[2,2,48,767]{3,2,1,0:T(8,128)(2,1)S(1)} collective-permute-done((bf16[2,2,48,767]{3,2,1,0:T(8,128)(2,1)S(1)}, bf16[2,2,48,767]{3,2,1,0:T(8,128)(2,1)S(1)}, u32[]{:S(2)}, u32[]{:S(2)}) %collective-permute-start.29) | collective-permute-done | bytes 294560 | tf_op jit(solution)/shard_map/ppermute | solution.py:108
  296.1 2.5 collective-permute-done.24
  302.9 2.9 collective-permute-start.31
  306.3 3.4 %collective-permute-start.26 = (bf16[48,767]{1,0:T(8,128)(2,1)S(1)}, bf16[48,767]{1,0:T(8,128)(2,1)S(1)}, u32[]{:S(2)}, u32[]{:S(2)}) collective-permute-start(bf16[48,767]{1,0:T(8,128)(2,1)S(1)} %fusion.67), channel_id=1, source_target_pairs={{0,2},{1,3},{2,0},{3,1},{4,6},{5,7},{6,4},{7,5},{8,10},{9,11},{10,... | collective-permute-start | bytes 220904 | tf_op jit(solution)/shard_map/ppermute | solution.py:108
  309.8 8.0 %collective-permute-done.31 = bf16[48,767]{1,0:T(8,128)(2,1)S(1)} collective-permute-done((bf16[48,767]{1,0:T(8,128)(2,1)S(1)}, bf16[48,767]{1,0:T(8,128)(2,1)S(1)}, u32[]{:S(2)}, u32[]{:S(2)}) %collective-permute-start.31) | collective-permute-done | bytes 73664 | tf_op jit(solution)/shard_map/ppermute | solution.py:108
  319.4 3.4 %collective-permute-start.43 = (bf16[96,767]{1,0:T(8,128)(2,1)S(1)}, bf16[96,767]{1,0:T(8,128)(2,1)S(1)}, u32[]{:S(2)}, u32[]{:S(2)}) collective-permute-start(bf16[96,767]{1,0:T(8,128)(2,1)S(1)} %fusion.66), channel_id=1, source_target_pairs={{0,2},{1,3},{2,0},{3,1},{4,6},{5,7},{6,4},{7,5},{8,10},{9,11},{10,... | collective-permute-start | bytes 441800 | tf_op jit(solution)/shard_map/ppermute | solution.py:108
  323.0 10.6 %collective-permute-done.43 = bf16[96,767]{1,0:T(8,128)(2,1)S(1)} collective-permute-done((bf16[96,767]{1,0:T(8,128)(2,1)S(1)}, bf16[96,767]{1,0:T(8,128)(2,1)S(1)}, u32[]{:S(2)}, u32[]{:S(2)}) %collective-permute-start.43) | collective-permute-done | bytes 147296 | tf_op jit(solution)/shard_map/ppermute | solution.py:108
  (348 shorter events, 101.6 us)
Async XLA Ops:
  3.7 28.7 %collective-permute-start = (bf16[128,767]{1,0:T(8,128)(2,1)S(1)}, bf16[128,767]{1,0:T(8,128)(2,1)S(1)}, u32[]{:S(2)}, u32[]{:S(2)}) collective-permute-start(bf16[128,767]{1,0:T(8,128)(2,1)S(1)} %bitcast.221), channel_id=1, source_target_pairs={{0,4},{4,0},{8,12},{12,8},{16,20},{20,16},{24,28},{28,24},{1,5},{5... | collective-permute-start | bytes 589064 | tf_op jit(solution)/shard_map/ppermute | solution.py:108
  5.9 42.4 %collective-permute-start.9 = (bf16[128,767]{1,0:T(8,128)(2,1)S(1)}, bf16[128,767]{1,0:T(8,128)(2,1)}, u32[]{:S(2)}, u32[]{:S(2)}) collective-permute-start(bf16[128,767]{1,0:T(8,128)(2,1)S(1)} %bitcast.220), channel_id=1, source_target_pairs={{0,4},{4,0},{8,12},{12,8},{16,20},{20,16},{24,28},{28,24},{1,5},{5... | collective-permute-start | bytes 589064 | tf_op jit(solution)/shard_map/ppermute | solution.py:108
  7.0 47.0 %copy-start.50 = (s32[1024]{0:T(1024)}, s32[1024]{0:T(1024)S(1)}, u32[]{:S(2)}) copy-start(s32[1024]{0:T(1024)S(1)} %pad_clamp_fusion.1) | copy-start | bytes 12292
  32.4 40.5 %copy-start.13 = (bf16[128,767]{1,0:T(8,128)(2,1)}, bf16[128,767]{1,0:T(8,128)(2,1)S(1)}, u32[]{:S(2)}) copy-start(bf16[128,767]{1,0:T(8,128)(2,1)S(1)} %get-tuple-element.83) | copy-start | bytes 589060
  32.4 40.5 %copy-start.15 = (bf16[128,767]{1,0:T(8,128)(2,1)}, bf16[128,767]{1,0:T(8,128)(2,1)S(1)}, u32[]{:S(2)}) copy-start(bf16[128,767]{1,0:T(8,128)(2,1)S(1)} %get-tuple-element.84) | copy-start | bytes 589060
  32.5 12.4 %collective-permute-start.2 = (bf16[256,767]{1,0:T(8,128)(2,1)S(1)}, bf16[256,767]{1,0:T(8,128)(2,1)S(1)}, u32[]{:S(2)}, u32[]{:S(2)}) collective-permute-start(bf16[256,767]{1,0:T(8,128)(2,1)S(1)} %get-tuple-element.82), channel_id=1, source_target_pairs={{0,16},{4,20},{8,24},{12,28},{16,0},{20,4},{24,8},{28,12},{1,17},{... | collective-permute-start | bytes 1178120 | tf_op jit(solution)/shard_map/ppermute | solution.py:108
  35.5 11.2 %collective-permute-start.1 = (bf16[256,767]{1,0:T(8,128)(2,1)S(1)}, bf16[256,767]{1,0:T(8,128)(2,1)S(1)}, u32[]{:S(2)}, u32[]{:S(2)}) collective-permute-start(bf16[256,767]{1,0:T(8,128)(2,1)S(1)} %get-tuple-element.82), channel_id=1, source_target_pairs={{0,8},{4,12},{8,0},{12,4},{16,24},{20,28},{24,16},{28,20},{1,9},{5... | collective-permute-start | bytes 1178120 | tf_op jit(solution)/shard_map/ppermute | solution.py:108
  44.9 6.4 %collective-permute-start.3 = (bf16[128,767]{1,0:T(8,128)(2,1)S(1)}, bf16[128,767]{1,0:T(8,128)(2,1)S(1)}, u32[]{:S(2)}, u32[]{:S(2)}) collective-permute-start(bf16[128,767]{1,0:T(8,128)(2,1)S(1)} %slice.149), channel_id=1, source_target_pairs={{0,8},{4,12},{8,0},{12,4},{16,24},{20,28},{24,16},{28,20},{1,9},{5... | collective-permute-start | bytes 589064 | tf_op jit(solution)/shard_map/ppermute | solution.py:108
  46.7 5.9 %collective-permute-start.4 = (bf16[128,767]{1,0:T(8,128)(2,1)S(1)}, bf16[128,767]{1,0:T(8,128)(2,1)S(1)}, u32[]{:S(2)}, u32[]{:S(2)}) collective-permute-start(bf16[128,767]{1,0:T(8,128)(2,1)S(1)} %slice.150), channel_id=1, source_target_pairs={{0,16},{4,20},{8,24},{12,28},{16,0},{20,4},{24,8},{28,12},{1,17},{... | collective-permute-start | bytes 589064 | tf_op jit(solution)/shard_map/ppermute | solution.py:108
  49.2 57.2 %copy-start.20 = (bf16[128,767]{1,0:T(8,128)(2,1)}, bf16[128,767]{1,0:T(8,128)(2,1)S(1)}, u32[]{:S(2)}) copy-start(bf16[128,767]{1,0:T(8,128)(2,1)S(1)} %get-tuple-element.77) | copy-start | bytes 589060
  50.1 181.0 %collective-permute-start.39 = (bf16[256,767]{1,0:T(8,128)(2,1)}, bf16[256,767]{1,0:T(8,128)(2,1)}, u32[]{:S(2)}, u32[]{:S(2)}) collective-permute-start(bf16[256,767]{1,0:T(8,128)(2,1)} %pad_maximum_fusion.4), channel_id=1, source_target_pairs={{0,4},{4,0},{8,12},{12,8},{16,20},{20,16},{24,28},{28,24},{1,5},{5... | collective-permute-start | bytes 1178120 | tf_op jit(solution)/shard_map/ppermute | solution.py:108
  65.3 6.2 %collective-permute-start.7 = (bf16[256,192]{1,0:T(8,128)(2,1)S(1)}, bf16[256,192]{1,0:T(8,128)(2,1)S(1)}, u32[]{:S(2)}, u32[]{:S(2)}) collective-permute-start(bf16[256,192]{1,0:T(8,128)(2,1)S(1)} %get-tuple-element.67), channel_id=1, source_target_pairs={{0,24},{4,28},{8,16},{12,20},{16,8},{20,12},{24,0},{28,4},{1,25},{... | collective-permute-start | bytes 294920 | tf_op jit(solution)/shard_map/ppermute | solution.py:108
  66.9 5.9 %collective-permute-start.6 = (bf16[256,192]{1,0:T(8,128)(2,1)S(1)}, bf16[256,192]{1,0:T(8,128)(2,1)S(1)}, u32[]{:S(2)}, u32[]{:S(2)}) collective-permute-start(bf16[256,192]{1,0:T(8,128)(2,1)S(1)} %get-tuple-element.68), channel_id=1, source_target_pairs={{0,16},{4,20},{8,24},{12,28},{16,0},{20,4},{24,8},{28,12},{1,17},{... | collective-permute-start | bytes 294920 | tf_op jit(solution)/shard_map/ppermute | solution.py:108
  68.0 5.0 %collective-permute-start.5 = (bf16[256,192]{1,0:T(8,128)(2,1)S(1)}, bf16[256,192]{1,0:T(8,128)(2,1)S(1)}, u32[]{:S(2)}, u32[]{:S(2)}) collective-permute-start(bf16[256,192]{1,0:T(8,128)(2,1)S(1)} %get-tuple-element.69), channel_id=1, source_target_pairs={{0,8},{4,12},{8,0},{12,4},{16,24},{20,28},{24,16},{28,20},{1,9},{5... | collective-permute-start | bytes 294920 | tf_op jit(solution)/shard_map/ppermute | solution.py:108
  106.5 62.7 %collective-permute-start.8 = (bf16[128,767]{1,0:T(8,128)(2,1)}, bf16[128,767]{1,0:T(8,128)(2,1)}, u32[]{:S(2)}, u32[]{:S(2)}) collective-permute-start(bf16[128,767]{1,0:T(8,128)(2,1)} %get-tuple-element.80), channel_id=1, source_target_pairs={{0,4},{4,0},{8,12},{12,8},{16,20},{20,16},{24,28},{28,24},{1,5},{5... | collective-permute-start | bytes 589064 | tf_op jit(solution)/shard_map/ppermute | solution.py:108
  113.3 37.4 %collective-permute-start.12 = (bf16[256,192]{0,1:T(8,128)(2,1)}, bf16[256,192]{0,1:T(8,128)(2,1)S(1)}, u32[]{:S(2)}, u32[]{:S(2)}) collective-permute-start(bf16[256,192]{0,1:T(8,128)(2,1)} %get-tuple-element.74), channel_id=1, source_target_pairs={{0,24},{4,28},{8,16},{12,20},{16,8},{20,12},{24,0},{28,4},{1,25},{... | collective-permute-start | bytes 294920 | tf_op jit(solution)/shard_map/ppermute | solution.py:108
  115.2 35.5 %collective-permute-start.11 = (bf16[256,192]{0,1:T(8,128)(2,1)}, bf16[256,192]{0,1:T(8,128)(2,1)}, u32[]{:S(2)}, u32[]{:S(2)}) collective-permute-start(bf16[256,192]{0,1:T(8,128)(2,1)} %get-tuple-element.75), channel_id=1, source_target_pairs={{0,16},{4,20},{8,24},{12,28},{16,0},{20,4},{24,8},{28,12},{1,17},{... | collective-permute-start | bytes 294920 | tf_op jit(solution)/shard_map/ppermute | solution.py:108
  116.0 34.7 %collective-permute-start.10 = (bf16[256,192]{0,1:T(8,128)(2,1)S(1)}, bf16[256,192]{0,1:T(8,128)(2,1)}, u32[]{:S(2)}, u32[]{:S(2)}) collective-permute-start(bf16[256,192]{0,1:T(8,128)(2,1)S(1)} %get-tuple-element.76), channel_id=1, source_target_pairs={{0,8},{4,12},{8,0},{12,4},{16,24},{20,28},{24,16},{28,20},{1,9},{5... | collective-permute-start | bytes 294920 | tf_op jit(solution)/shard_map/ppermute | solution.py:108
  165.3 11.1 %collective-permute-start.15 = (bf16[256,576]{0,1:T(8,128)(2,1)}, bf16[256,576]{0,1:T(8,128)(2,1)S(1)}, u32[]{:S(2)}, u32[]{:S(2)}) collective-permute-start(bf16[256,576]{0,1:T(8,128)(2,1)} %get-tuple-element.63), channel_id=1, source_target_pairs={{0,24},{4,28},{8,16},{12,20},{16,8},{20,12},{24,0},{28,4},{1,25},{... | collective-permute-start | bytes 884744 | tf_op jit(solution)/shard_map/ppermute | solution.py:108
  167.2 14.2 %collective-permute-start.14 = (bf16[256,576]{0,1:T(8,128)(2,1)}, bf16[256,576]{0,1:T(8,128)(2,1)}, u32[]{:S(2)}, u32[]{:S(2)}) collective-permute-start(bf16[256,576]{0,1:T(8,128)(2,1)} %get-tuple-element.64), channel_id=1, source_target_pairs={{0,16},{4,20},{8,24},{12,28},{16,0},{20,4},{24,8},{28,12},{1,17},{... | collective-permute-start | bytes 884744 | tf_op jit(solution)/shard_map/ppermute | solution.py:108
  168.0 13.4 %collective-permute-start.13 = (bf16[256,576]{0,1:T(8,128)(2,1)}, bf16[256,576]{0,1:T(8,128)(2,1)}, u32[]{:S(2)}, u32[]{:S(2)}) collective-permute-start(bf16[256,576]{0,1:T(8,128)(2,1)} %get-tuple-element.65), channel_id=1, source_target_pairs={{0,8},{4,12},{8,0},{12,4},{16,24},{20,28},{24,16},{28,20},{1,9},{5... | collective-permute-start | bytes 884744 | tf_op jit(solution)/shard_map/ppermute | solution.py:108
  169.1 66.7 %collective-permute-start.32 = (bf16[256,1536]{0,1:T(8,128)(2,1)}, bf16[256,1536]{0,1:T(8,128)(2,1)}, u32[]{:S(2)}, u32[]{:S(2)}) collective-permute-start(bf16[256,1536]{0,1:T(8,128)(2,1)} %bitcast.77), channel_id=1, source_target_pairs={{0,4},{4,0},{8,12},{12,8},{16,20},{20,16},{24,28},{28,24},{1,5},{5... | collective-permute-start | bytes 2359304 | tf_op jit(solution)/shard_map/ppermute | solution.py:108
  176.3 55.4 %collective-permute-start.38 = (bf16[256,1536]{0,1:T(8,128)(2,1)}, bf16[256,1536]{0,1:T(8,128)(2,1)}, u32[]{:S(2)}, u32[]{:S(2)}) collective-permute-start(bf16[256,1536]{0,1:T(8,128)(2,1)} %bitcast.218), channel_id=1, source_target_pairs={{0,4},{4,0},{8,12},{12,8},{16,20},{20,16},{24,28},{28,24},{1,5},{5... | collective-permute-start | bytes 2359304 | tf_op jit(solution)/shard_map/ppermute | solution.py:108
  194.5 2.6 collective-permute-start.17
  196.6 31.4 %collective-permute-start.16 = (bf16[128,767]{1,0:T(8,128)(2,1)S(1)}, bf16[128,767]{1,0:T(8,128)(2,1)S(1)}, u32[]{:S(2)}, u32[]{:S(2)}) collective-permute-start(bf16[128,767]{1,0:T(8,128)(2,1)S(1)} %get-tuple-element.72), channel_id=1, source_target_pairs={{0,4},{4,0},{8,12},{12,8},{16,20},{20,16},{24,28},{28,24},{1,5},{5... | collective-permute-start | bytes 589064 | tf_op jit(solution)/shard_map/ppermute | solution.py:108
  197.7 13.4 %collective-permute-start.18 = (f32[64,128]{1,0:T(8,128)S(1)}, f32[64,128]{1,0:T(8,128)S(1)}, u32[]{:S(2)}, u32[]{:S(2)}) collective-permute-start(f32[64,128]{1,0:T(8,128)S(1)} %fusion.86), channel_id=1, source_target_pairs={{0,8},{4,12},{8,0},{12,4},{16,24},{20,28},{24,16},{28,20},{1,9},{5... | collective-permute-start | bytes 98312 | tf_op jit(solution)/shard_map/ppermute | solution.py:108
  211.2 5.8 %collective-permute-start.19 = (f32[64,128]{1,0:T(8,128)S(1)}, f32[64,128]{1,0:T(8,128)S(1)}, u32[]{:S(2)}, u32[]{:S(2)}) collective-permute-start(f32[64,128]{1,0:T(8,128)S(1)} %fusion.105), channel_id=1, source_target_pairs={{0,16},{4,20},{8,24},{12,28},{16,0},{20,4},{24,8},{28,12},{1,17},{... | collective-permute-start | bytes 98312 | tf_op jit(solution)/shard_map/ppermute | solution.py:108
  217.0 4.0 %collective-permute-start.20 = (f32[64,128]{1,0:T(8,128)S(1)}, f32[64,128]{1,0:T(8,128)S(1)}, u32[]{:S(2)}, u32[]{:S(2)}) collective-permute-start(f32[64,128]{1,0:T(8,128)S(1)} %add.376), channel_id=1, source_target_pairs={{0,1},{1,0},{2,3},{3,2},{4,5},{5,4},{6,7},{7,6},{8,9},{9,8},{10,11... | collective-permute-start | bytes 98312 | tf_op jit(solution)/shard_map/ppermute | solution.py:108
  221.1 4.9 %collective-permute-start.21 = (f32[64,128]{1,0:T(8,128)S(1)}, f32[64,128]{1,0:T(8,128)S(1)}, u32[]{:S(2)}, u32[]{:S(2)}) collective-permute-start(f32[64,128]{1,0:T(8,128)S(1)} %add.377), channel_id=1, source_target_pairs={{0,2},{1,3},{2,0},{3,1},{4,6},{5,7},{6,4},{7,5},{8,10},{9,11},{10,... | collective-permute-start | bytes 98312 | tf_op jit(solution)/shard_map/ppermute | solution.py:108
  226.0 14.1 %collective-permute-start.27 = (bf16[2,2,2,2,48,767]{5,4,3,2,1,0:T(8,128)(2,1)}, bf16[2,2,2,2,48,767]{5,4,3,2,1,0:T(8,128)(2,1)}, u32[]{:S(2)}, u32[]{:S(2)}) collective-permute-start(bf16[2,2,2,2,48,767]{5,4,3,2,1,0:T(8,128)(2,1)} %fusion.29), channel_id=1, source_target_pairs={{0,4},{4,0},{8,12},{12,8},{16,20},{20,16},{24,28},{28,24},{1,5},{5... | collective-permute-start | bytes 3534344 | tf_op jit(solution)/shard_map/ppermute | solution.py:108
  228.0 7.8 %collective-permute-start.33 = (bf16[256,767]{1,0:T(8,128)(2,1)}, bf16[256,767]{1,0:T(8,128)(2,1)}, u32[]{:S(2)}, u32[]{:S(2)}) collective-permute-start(bf16[256,767]{1,0:T(8,128)(2,1)} %multiply_convert_fusion.1), channel_id=1, source_target_pairs={{0,4},{4,0},{8,12},{12,8},{16,20},{20,16},{24,28},{28,24},{1,5},{5... | collective-permute-start | bytes 1178120 | tf_op jit(solution)/shard_map/ppermute | solution.py:108
  231.1 11.8 %collective-permute-start.22 = (bf16[2,2,2,2,48,767]{5,4,2,3,0,1:T(8,128)(2,1)}, bf16[2,2,2,2,48,767]{5,4,2,3,0,1:T(8,128)(2,1)S(1)}, u32[]{:S(2)}, u32[]{:S(2)}) collective-permute-start(bf16[2,2,2,2,48,767]{5,4,2,3,0,1:T(8,128)(2,1)} %fusion.26), channel_id=1, source_target_pairs={{0,4},{4,0},{8,12},{12,8},{16,20},{20,16},{24,28},{28,24},{1,5},{5... | collective-permute-start | bytes 3534344 | tf_op jit(solution)/shard_map/ppermute | solution.py:108
  234.7 28.9 %collective-permute-start.40 = (bf16[2,2,2,96,767]{4,3,1,2,0:T(8,128)(2,1)S(1)}, bf16[2,2,2,96,767]{4,3,1,2,0:T(8,128)(2,1)S(1)}, u32[]{:S(2)}, u32[]{:S(2)}) collective-permute-start(bf16[2,2,2,96,767]{4,3,1,2,0:T(8,128)(2,1)S(1)} %fusion.28), channel_id=1, source_target_pairs={{0,8},{4,12},{8,0},{12,4},{16,24},{20,28},{24,16},{28,20},{1,9},{5... | collective-permute-start | bytes 3534344 | tf_op jit(solution)/shard_map/ppermute | solution.py:108
  239.0 28.9 %collective-permute-start.34 = (bf16[2,2,2,96,767]{4,3,1,2,0:T(8,128)(2,1)S(1)}, bf16[2,2,2,96,767]{4,3,1,2,0:T(8,128)(2,1)S(1)}, u32[]{:S(2)}, u32[]{:S(2)}) collective-permute-start(bf16[2,2,2,96,767]{4,3,1,2,0:T(8,128)(2,1)S(1)} %fusion.27), channel_id=1, source_target_pairs={{0,16},{4,20},{8,24},{12,28},{16,0},{20,4},{24,8},{28,12},{1,17},{... | collective-permute-start | bytes 3534344 | tf_op jit(solution)/shard_map/ppermute | solution.py:108
  241.9 38.6 %collective-permute-start.28 = (bf16[2,2,2,48,767]{4,3,2,1,0:T(8,128)(2,1)S(1)}, bf16[2,2,2,48,767]{4,3,2,1,0:T(8,128)(2,1)S(1)}, u32[]{:S(2)}, u32[]{:S(2)}) collective-permute-start(bf16[2,2,2,48,767]{4,3,2,1,0:T(8,128)(2,1)S(1)} %fusion.49), channel_id=1, source_target_pairs={{0,16},{4,20},{8,24},{12,28},{16,0},{20,4},{24,8},{28,12},{1,17},{... | collective-permute-start | bytes 1767176 | tf_op jit(solution)/shard_map/ppermute | solution.py:108
  243.3 38.5 %collective-permute-start.23 = (bf16[2,2,2,48,767]{4,3,1,2,0:T(8,128)(2,1)S(1)}, bf16[2,2,2,48,767]{4,3,1,2,0:T(8,128)(2,1)S(1)}, u32[]{:S(2)}, u32[]{:S(2)}) collective-permute-start(bf16[2,2,2,48,767]{4,3,1,2,0:T(8,128)(2,1)S(1)} %fusion.48), channel_id=1, source_target_pairs={{0,8},{4,12},{8,0},{12,4},{16,24},{20,28},{24,16},{28,20},{1,9},{5... | collective-permute-start | bytes 1767176 | tf_op jit(solution)/shard_map/ppermute | solution.py:108
  264.0 36.3 %collective-permute-start.41 = (bf16[2,2,96,767]{3,2,0,1:T(8,128)(2,1)S(1)}, bf16[2,2,96,767]{3,2,0,1:T(8,128)(2,1)S(1)}, u32[]{:S(2)}, u32[]{:S(2)}) collective-permute-start(bf16[2,2,96,767]{3,2,0,1:T(8,128)(2,1)S(1)} %fusion.51), channel_id=1, source_target_pairs={{0,16},{4,20},{8,24},{12,28},{16,0},{20,4},{24,8},{28,12},{1,17},{... | collective-permute-start | bytes 1767176 | tf_op jit(solution)/shard_map/ppermute | solution.py:108
  268.2 32.8 %collective-permute-start.35 = (bf16[2,2,96,767]{3,2,0,1:T(8,128)(2,1)S(1)}, bf16[2,2,96,767]{3,2,0,1:T(8,128)(2,1)S(1)}, u32[]{:S(2)}, u32[]{:S(2)}) collective-permute-start(bf16[2,2,96,767]{3,2,0,1:T(8,128)(2,1)S(1)} %fusion.50), channel_id=1, source_target_pairs={{0,8},{4,12},{8,0},{12,4},{16,24},{20,28},{24,16},{28,20},{1,9},{5... | collective-permute-start | bytes 1767176 | tf_op jit(solution)/shard_map/ppermute | solution.py:108
  280.7 13.6 %collective-permute-start.29 = (bf16[2,2,48,767]{3,2,1,0:T(8,128)(2,1)S(1)}, bf16[2,2,48,767]{3,2,1,0:T(8,128)(2,1)S(1)}, u32[]{:S(2)}, u32[]{:S(2)}) collective-permute-start(bf16[2,2,48,767]{3,2,1,0:T(8,128)(2,1)S(1)} %fusion.57), channel_id=1, source_target_pairs={{0,8},{4,12},{8,0},{12,4},{16,24},{20,28},{24,16},{28,20},{1,9},{5... | collective-permute-start | bytes 883592 | tf_op jit(solution)/shard_map/ppermute | solution.py:108
  282.0 16.5 %collective-permute-start.24 = (bf16[2,2,48,767]{3,2,0,1:T(8,128)(2,1)S(1)}, bf16[2,2,48,767]{3,2,0,1:T(8,128)(2,1)S(1)}, u32[]{:S(2)}, u32[]{:S(2)}) collective-permute-start(bf16[2,2,48,767]{3,2,0,1:T(8,128)(2,1)S(1)} %fusion.56), channel_id=1, source_target_pairs={{0,16},{4,20},{8,24},{12,28},{16,0},{20,4},{24,8},{28,12},{1,17},{... | collective-permute-start | bytes 883592 | tf_op jit(solution)/shard_map/ppermute | solution.py:108
  294.4 8.4 %collective-permute-start.30 = (bf16[2,48,767]{2,1,0:T(8,128)(2,1)S(1)}, bf16[2,48,767]{2,1,0:T(8,128)(2,1)S(1)}, u32[]{:S(2)}, u32[]{:S(2)}) collective-permute-start(bf16[2,48,767]{2,1,0:T(8,128)(2,1)S(1)} %fusion.64), channel_id=1, source_target_pairs={{0,1},{1,0},{2,3},{3,2},{4,5},{5,4},{6,7},{7,6},{8,9},{9,8},{10,11... | collective-permute-start | bytes 441800 | tf_op jit(solution)/shard_map/ppermute | solution.py:108
  298.6 7.6 %collective-permute-start.25 = (bf16[2,48,767]{2,1,0:T(8,128)(2,1)S(1)}, bf16[2,48,767]{2,1,0:T(8,128)(2,1)S(1)}, u32[]{:S(2)}, u32[]{:S(2)}) collective-permute-start(bf16[2,48,767]{2,1,0:T(8,128)(2,1)S(1)} %fusion.63), channel_id=1, source_target_pairs={{0,1},{1,0},{2,3},{3,2},{4,5},{5,4},{6,7},{7,6},{8,9},{9,8},{10,11... | collective-permute-start | bytes 441800 | tf_op jit(solution)/shard_map/ppermute | solution.py:108
  300.5 18.8 %collective-permute-start.42 = (bf16[2,96,767]{2,1,0:T(8,128)(2,1)S(1)}, bf16[2,96,767]{2,1,0:T(8,128)(2,1)S(1)}, u32[]{:S(2)}, u32[]{:S(2)}) collective-permute-start(bf16[2,96,767]{2,1,0:T(8,128)(2,1)S(1)} %fusion.59), channel_id=1, source_target_pairs={{0,1},{1,0},{2,3},{3,2},{4,5},{5,4},{6,7},{7,6},{8,9},{9,8},{10,11... | collective-permute-start | bytes 883592 | tf_op jit(solution)/shard_map/ppermute | solution.py:108
  301.2 21.6 %collective-permute-start.36 = (bf16[2,96,767]{2,1,0:T(8,128)(2,1)S(1)}, bf16[2,96,767]{2,1,0:T(8,128)(2,1)S(1)}, u32[]{:S(2)}, u32[]{:S(2)}) collective-permute-start(bf16[2,96,767]{2,1,0:T(8,128)(2,1)S(1)} %fusion.58), channel_id=1, source_target_pairs={{0,1},{1,0},{2,3},{3,2},{4,5},{5,4},{6,7},{7,6},{8,9},{9,8},{10,11... | collective-permute-start | bytes 883592 | tf_op jit(solution)/shard_map/ppermute | solution.py:108
  302.9 14.9 %collective-permute-start.31 = (bf16[48,767]{1,0:T(8,128)(2,1)S(1)}, bf16[48,767]{1,0:T(8,128)(2,1)S(1)}, u32[]{:S(2)}, u32[]{:S(2)}) collective-permute-start(bf16[48,767]{1,0:T(8,128)(2,1)S(1)} %fusion.68), channel_id=1, source_target_pairs={{0,2},{1,3},{2,0},{3,1},{4,6},{5,7},{6,4},{7,5},{8,10},{9,11},{10,... | collective-permute-start | bytes 220904 | tf_op jit(solution)/shard_map/ppermute | solution.py:108
  306.3 12.2 %collective-permute-start.26 = (bf16[48,767]{1,0:T(8,128)(2,1)S(1)}, bf16[48,767]{1,0:T(8,128)(2,1)S(1)}, u32[]{:S(2)}, u32[]{:S(2)}) collective-permute-start(bf16[48,767]{1,0:T(8,128)(2,1)S(1)} %fusion.67), channel_id=1, source_target_pairs={{0,2},{1,3},{2,0},{3,1},{4,6},{5,7},{6,4},{7,5},{8,10},{9,11},{10,... | collective-permute-start | bytes 220904 | tf_op jit(solution)/shard_map/ppermute | solution.py:108
  319.4 14.3 %collective-permute-start.43 = (bf16[96,767]{1,0:T(8,128)(2,1)S(1)}, bf16[96,767]{1,0:T(8,128)(2,1)S(1)}, u32[]{:S(2)}, u32[]{:S(2)}) collective-permute-start(bf16[96,767]{1,0:T(8,128)(2,1)S(1)} %fusion.66), channel_id=1, source_target_pairs={{0,2},{1,3},{2,0},{3,1},{4,6},{5,7},{6,4},{7,5},{8,10},{9,11},{10,... | collective-permute-start | bytes 441800 | tf_op jit(solution)/shard_map/ppermute | solution.py:108
  322.9 12.3 %collective-permute-start.37 = (bf16[96,767]{1,0:T(8,128)(2,1)S(1)}, bf16[96,767]{1,0:T(8,128)(2,1)S(1)}, u32[]{:S(2)}, u32[]{:S(2)}) collective-permute-start(bf16[96,767]{1,0:T(8,128)(2,1)S(1)} %fusion.65), channel_id=1, source_target_pairs={{0,2},{1,3},{2,0},{3,1},{4,6},{5,7},{6,4},{7,5},{8,10},{9,11},{10,... | collective-permute-start | bytes 441800 | tf_op jit(solution)/shard_map/ppermute | solution.py:108
  (68 other events, 437.3 us)
